TPU v7x, 256 devices: a whole 4x4x8 slice. The times are simulated.
256 devices in a mesh: row: 16 (over y_lo, x, core), col: 16 (over y_hi, z).
Axes of the slice: x: 4, y: 4 (y_hi: 2, y_lo: 2; y = y_hi * 2 + y_lo), z: 8, core: 2. Of those that a mesh axis runs over, the one named last changes fastest.
Arguments:
- pair_tensor: float32 [512, 512, 128], P('row', 'col'), may hold values from -6 to 6
- norm_in_gain: float32 [2, 128], replicated, may hold values from 0.5 to 1.5
- norm_in_bias: float32 [2, 128], replicated, may hold values from -3 to 3
- proj_weight: bfloat16 [2, 128, 512], replicated, may hold values from -0.5 to 0.5
- gate_weight: bfloat16 [2, 128, 128], replicated, may hold values from -0.5 to 0.5
- norm_out_gain: float32 [2, 128], replicated, may hold values from 0.5 to 1.5
- norm_out_bias: float32 [2, 128], replicated, may hold values from -3 to 3
- out_weight: bfloat16 [2, 128, 128], replicated, may hold values from -0.5 to 0.5
Outputs:
- pair_out: float32 [512, 512, 128], P('row', 'col')
All inputs are finite; a program needn't handle non-finite values.
Results may differ from a plain program's by a relative error of at most 0.0023.
Values may be sent and summed in bfloat16 or wider, within the bound.
No kernel may reach another device: no remote copies, remote signals or barrier semaphores. Data moves between devices by JAX's collectives and lax.ppermute only.
A program may use at most 64 MiB of HBM per device.

v0:
```python
import functools

import jax
import jax.numpy as jnp
from jax import lax
from jax.experimental import pallas as pl
from jax.experimental.pallas import tpu as pltpu
from jax.sharding import Mesh, PartitionSpec as P

RH_ORDER = (1, 3, 2, 7, 0, 6, 4, 5)
COL_ORDER = (13, 14, 5, 11, 3, 7, 4, 15, 0, 6, 9, 8, 10, 1, 2, 12)
RANKS = [8 * col + rh for rh in RH_ORDER for col in COL_ORDER]
C = 128
EPS = 1e-05
VMEM_LIMIT = 48 * 1024 * 1024


def full(memory_space=pltpu.VMEM):
    return pl.BlockSpec(memory_space=memory_space)


def params():
    return pltpu.CompilerParams(vmem_limit_bytes=VMEM_LIMIT)


def norm_rows(x, gain_row, bias_row):
    centered = x - jnp.mean(x, axis=-1, keepdims=True)
    variance = jnp.mean(centered * centered, axis=-1, keepdims=True)
    return centered * lax.rsqrt(variance + EPS) * gain_row + bias_row


def dot(a, b, contract):
    return lax.dot_general(a, b, (contract, ((), ())), preferred_element_type=jnp.float32)


def emit_operands(z, s, gain_row, bias_row, proj, wide, normed_out):
    rows = z.reshape(256, C)
    normed = norm_rows(rows, gain_row, bias_row).astype(jnp.bfloat16)
    normed_out[s : s + 2] = normed.reshape(2, 128, C)
    projected = dot(proj, normed, ((0,), (1,)))
    left = jax.nn.sigmoid(projected[0:C]) * projected[C : 2 * C]
    right = jax.nn.sigmoid(projected[2 * C : 3 * C]) * projected[3 * C : 4 * C]
    for t in range(2):
        wide[s + t] = left[:, 128 * t : 128 * t + 128].astype(jnp.bfloat16)
        wide[8 + s + t] = right[:, 128 * t : 128 * t + 128].astype(jnp.bfloat16)


def write_gate(normed, gate_w, gate):
    values = dot(normed[...].reshape(1024, C), gate_w, ((1,), (0,)))
    gate[...] = jax.nn.sigmoid(values).reshape(8, 128, C)


def first_kernel(
    z_hbm, gain_in, bias_in, proj_hbm, gate_hbm, gain_out, bias_out,
    ops_ref, normed_ref, vec_ref, gate_w, z, proj, wide, sems,
):
    vectors = (gain_in, bias_in, gain_out, bias_out)
    pairs = [(z_hbm, z), (proj_hbm.at[0], proj)]
    pairs += [(ref, vec_ref.at[2 * i : 2 * i + 2]) for i, ref in enumerate(vectors)]
    pairs += [(gate_hbm, gate_w)]
    copies = [pltpu.make_async_copy(src, dst, sems.at[i]) for i, (src, dst) in enumerate(pairs)]
    for copy in copies:
        copy.start()
    for copy in copies:
        copy.wait()
    for s in range(0, 8, 2):
        rows = jnp.stack([z[:, s], z[:, s + 1]])
        emit_operands(rows, s, vec_ref[0:1], vec_ref[2:3], proj[...], wide, normed_ref)
    ops_ref[...] = jnp.swapaxes(wide[...], 0, 1)


def finish_kernel(layer, y_ref, z_ref, gate_ref, vec, out_w, *rest):
    if layer == 0:
        proj, z_out, ops_ref, normed_out, y32, wide = rest
    else:
        z_hbm, y32, z_out, sems = rest
    y32[...] = jnp.swapaxes(y_ref[...].astype(jnp.float32), 0, 1)
    gain = jnp.transpose(jnp.broadcast_to(vec[4 + layer : 5 + layer, :], (C, C)))
    bias = jnp.transpose(jnp.broadcast_to(vec[6 + layer : 7 + layer, :], (C, C)))
    weight = jnp.concatenate([out_w[layer], out_w[layer]])
    copies = []
    for s in range(0, 8, 2):
        new = []
        for t in (s, s + 1):
            tile = y32[t]
            centered = tile - jnp.mean(tile, axis=0, keepdims=True)
            scale = lax.rsqrt(jnp.mean(centered * centered, axis=0, keepdims=True) + EPS)
            normed = centered * scale * gain + bias
            high = normed.astype(jnp.bfloat16)
            low = (normed - high.astype(jnp.float32)).astype(jnp.bfloat16)
            both = jnp.concatenate([high, low])
            update = gate_ref[t] * dot(both, weight, ((0,), (0,)))
            value = z_ref[:, t] + update.reshape(4, 32, C)
            z_out[:, t] = value
            new.append(value)
        if layer == 0:
            emit_operands(jnp.stack(new), s, vec[1:2], vec[3:4], proj[1], wide, normed_out)
        elif s % 4 == 2:
            part = slice(s - 2, s + 2)
            copies.append(pltpu.make_async_copy(z_out.at[:, part], z_hbm.at[:, part], sems.at[s // 4]))
            copies[-1].start()
    if layer == 0:
        ops_ref[...] = jnp.swapaxes(wide[...], 0, 1)
    for copy in copies:
        copy.wait()


def swap_groups(tiles):
    lane = lax.broadcasted_iota(jnp.int32, tiles[0].shape, 1)
    low = lane < 64
    even = (lane // 32) % 2 == 0
    t0, t1, t2, t3 = tiles
    u0 = jnp.where(low, t0, pltpu.roll(t2, 64, 1))
    u2 = jnp.where(low, pltpu.roll(t0, 64, 1), t2)
    u1 = jnp.where(low, t1, pltpu.roll(t3, 64, 1))
    u3 = jnp.where(low, pltpu.roll(t1, 64, 1), t3)
    v0 = jnp.where(even, u0, pltpu.roll(u1, 32, 1))
    v1 = jnp.where(even, pltpu.roll(u0, 96, 1), u1)
    v2 = jnp.where(even, u2, pltpu.roll(u3, 32, 1))
    v3 = jnp.where(even, pltpu.roll(u2, 96, 1), u3)
    return v0, v1, v2, v3


def write_back(product, b, y_ref):
    for d, tile in enumerate(swap_groups([p.astype(jnp.bfloat16) for p in product])):
        y_ref[:, COL_ORDER.index(4 * b + d)] = tile.reshape(8, 8, 128)


def place(m, parity):
    even, odd = (COL_ORDER.index(2 * RH_ORDER[m] + i) for i in range(2))
    return even + parity * (odd - even)


def both_of(ref, n):
    both = ref[:, n].astype(jnp.float32)
    return both[:, 0:8].reshape(64, 128), both[:, 8:16].reshape(64, 128)


def outgoing_half(left, tiles, right, put):
    for b in range(4):
        for a, tile in enumerate(swap_groups(tiles[4 * b : 4 * b + 4])):
            right[:, 8 * a : 8 * a + 8, 128 * b : 128 * b + 128] = tile.reshape(8, 8, 128)
    rows = right[...].reshape(256, 512).astype(jnp.bfloat16)
    product = dot(left[...], rows, ((1,), (1,)))
    for b in range(2):
        parts = [product[64 * a : 64 * a + 64, 128 * b : 128 * b + 128] for a in range(4)]
        for d, tile in enumerate(swap_groups([p.astype(jnp.bfloat16) for p in parts])):
            put(4 * b + d, tile.reshape(8, 8, 128))


def outgoing_own(own, normed, gate_w, left, y_half, gate, right):
    write_gate(normed, gate_w[0], gate)
    tiles = [both_of(own, COL_ORDER.index(q)) for q in range(16)]
    for b in range(4):
        for a, tile in enumerate(swap_groups([t[0] for t in tiles[4 * b : 4 * b + 4]])):
            left[64 * a : 64 * a + 64, 128 * b : 128 * b + 128] = tile.astype(jnp.bfloat16)

    def put(m, tile):
        y_half[m] = tile

    outgoing_half(left, [t[1] for t in tiles], right, put)


def outgoing_other(core_ref, other, left, y_half, y_ref, right):
    core = core_ref[0]
    for m in range(8):
        y_ref[:, place(m, core)] = y_half[m]

    def put(m, tile):
        y_ref[:, place(m, 1 - core)] = tile

    tiles = [other[:, COL_ORDER.index(q)].astype(jnp.float32).reshape(64, 128) for q in range(16)]
    outgoing_half(left, tiles, right, put)


def incoming_half(core, ref, left, right):
    for b in range(4):
        lanes = slice(128 * b, 128 * b + 128)
        for a, tile in enumerate(swap_groups([both_of(ref, COL_ORDER.index(q))[1] for q in range(4 * b, 4 * b + 4)])):
            right[64 * a : 64 * a + 64, lanes] = tile.astype(jnp.bfloat16)
    for b in range(2):
        lanes = slice(128 * b, 128 * b + 128)
        picks = [both_of(ref, place(m, core))[0] for m in range(4 * b, 4 * b + 4)]
        for a, tile in enumerate(swap_groups(picks)):
            left[64 * a : 64 * a + 64, lanes] = tile.astype(jnp.bfloat16)
    return dot(left[...], right[...], ((0,), (0,)))


def incoming_own(core_ref, own, normed, gate_w, partial, gate, left, right):
    write_gate(normed, gate_w[1], gate)
    partial[...] = incoming_half(core_ref[0], own, left, right)


def incoming_other(core_ref, other, partial, y_ref, left, right):
    product = partial[...] + incoming_half(core_ref[0], other, left, right)
    product = product.reshape(8, 4, 8, 512)
    for b in range(4):
        parts = [product[:, a, :, 128 * b : 128 * b + 128].reshape(64, 128) for a in range(4)]
        write_back(parts, b, y_ref)


def call(kernel, inputs, outputs, scratch, flops):
    smem = [full(pltpu.SMEM) if v.shape == (1,) else full() for v in inputs]
    return pl.pallas_call(
        kernel,
        out_shape=outputs,
        in_specs=smem,
        out_specs=jax.tree.map(lambda _: full(), outputs),
        scratch_shapes=scratch,
        compiler_params=params(),
        cost_estimate=pl.CostEstimate(flops=flops, bytes_accessed=2 << 20, transcendentals=0),
    )(*inputs)


def local(z, gain_in, bias_in, proj, gate_w, gain_out, bias_out, out_w):
    core = lax.axis_index("core").astype(jnp.int32).reshape(1)
    swap = ((0, 1), (1, 0))
    exchange = functools.partial(
        lax.all_to_all,
        axis_name=("yh", "z", "yl", "x"),
        split_axis=0,
        concat_axis=0,
        axis_index_groups=[RANKS],
        tiled=True,
    )
    z4 = z.reshape(4, 8, 32, C)
    shape = jax.ShapeDtypeStruct
    ops_shape = jax.ShapeDtypeStruct((C, 16, 128), jnp.bfloat16)
    normed_shape = shape((8, 128, C), jnp.bfloat16)
    gate_shape = jax.ShapeDtypeStruct((8, 128, C), jnp.float32)
    z_shape = jax.ShapeDtypeStruct((4, 8, 32, C), jnp.float32)
    wide = pltpu.VMEM((16, C, 128), jnp.bfloat16)
    y32 = pltpu.VMEM((8, C, 128), jnp.float32)

    operands = [pltpu.with_memory_space_constraint(v, pltpu.HBM) for v in (z4, gain_in, bias_in, proj, gate_w, gain_out, bias_out)]
    ops, normed, vec, gate_w = pl.pallas_call(
        first_kernel,
        out_shape=(ops_shape, normed_shape, shape((8, C), jnp.float32), shape((2, C, C), jnp.bfloat16)),
        in_specs=[full(pltpu.HBM)] * 7,
        out_specs=(full(), full(), full(), full()),
        scratch_shapes=[
            pltpu.VMEM((4, 8, 32, C), jnp.float32),
            pltpu.VMEM((C, 4 * C), jnp.bfloat16),
            wide,
            pltpu.SemaphoreType.DMA((7,)),
        ],
        compiler_params=params(),
    )(*operands)

    own = exchange(ops).reshape(8, 16, 16, 128)
    other = lax.ppermute(own[:, :, 8:], "core", swap)
    half = 2 * 256 * 256 * 512
    rows = [pltpu.VMEM((8, 32, 512), jnp.float32)]
    outputs = (shape((256, 512), jnp.bfloat16), shape((8, 8, 8, 128), jnp.bfloat16), gate_shape)
    left, y_half, gate = call(outgoing_own, (own, normed, gate_w), outputs, rows, half)
    outputs = shape((8, 16, 8, 128), jnp.bfloat16)
    y = call(outgoing_other, (core, other, left, y_half), outputs, rows, half)
    y = exchange(y.reshape(C, 8, 128))

    z4, ops, normed = pl.pallas_call(
        functools.partial(finish_kernel, 0),
        out_shape=(z_shape, ops_shape, normed_shape),
        in_specs=[full()] * 6,
        out_specs=(full(), full(), full()),
        scratch_shapes=[y32, wide],
        compiler_params=params(),
    )(y, z4, gate, vec, out_w, proj)

    own = exchange(ops).reshape(8, 16, 16, 128)
    other = lax.ppermute(own, "core", swap)
    sides = [pltpu.VMEM((256, 256), jnp.bfloat16), pltpu.VMEM((256, 512), jnp.bfloat16)]
    outputs = (shape((256, 512), jnp.float32), gate_shape)
    partial, gate = call(incoming_own, (core, own, normed, gate_w), outputs, sides, half)
    y = call(incoming_other, (core, other, partial), shape((8, 16, 8, 128), jnp.bfloat16), sides, half)
    y = exchange(y.reshape(C, 8, 128))

    out = pl.pallas_call(
        functools.partial(finish_kernel, 1),
        out_shape=z_shape,
        in_specs=[full()] * 5,
        out_specs=full(pltpu.HBM),
        scratch_shapes=[y32, pltpu.VMEM((4, 8, 32, C), jnp.float32), pltpu.SemaphoreType.DMA((2,))],
        compiler_params=params(),
    )(y, z4, gate, vec, out_w)
    return out.reshape(32, 32, C)


def solution(mesh):
    fine = Mesh(mesh.devices.reshape(2, 4, 2, 2, 8), ("yl", "x", "core", "yh", "z"))
    block = P(("yl", "x", "core"), ("yh", "z"), None)
    return jax.shard_map(
        local,
        mesh=fine,
        in_specs=(block, P(), P(), P(), P(), P(), P(), P()),
        out_specs=block,
        check_vma=False,
    )
```

profile of v0, /device:TPU:1, one launch (start us, length us, event | category | flops | bytes accessed | tf_op | source)
XLA Modules:
  0.0 105.5 jit_solution(7165517049726734604)
XLA Ops:
  0.0 1.9 %shard_map.82 = (bf16[128,16,128]{2,1,0:T(8,128)(2,1)S(1)}, bf16[8,128,128]{2,1,0:T(8,128)(2,1)S(1)}, f32[8,128]{1,0:T(8,128)S(1)}, bf16[2,128,128]{2,1,0:T(8,128)(2,1)S(1)}) custom-call(f32[4,8,32,128]{3,2,1,0:T(8,128)} %bitcast.9, f32[2,128]{1,0:T(2,128)} %gain_in.1, f32[2,128]{1,0:T(2,128)} %bias_in.1, bf16[2,128,512]{2,1,0:T(8,128)(2,1)} %rest_0_.1, ...), custom_call_target="tpu_custom_call" | custom-call | tf_op jit(solution)/shard_map/pallas_call | solution.py:236
  1.9 30.3 %all_to_all.20 = bf16[128,16,128]{2,1,0:T(8,128)(2,1)S(1)} all-to-all(bf16[128,16,128]{2,1,0:T(8,128)(2,1)S(1)} %get-tuple-element.17), channel_id=1, replica_groups={{45,46,37,43,35,39,36,47,32,38,41,40,42,33,34,44,109,110,101,107,99,103..., dimensions={0} | all-to-all | bytes 1048576 | tf_op jit(solution)/shard_map/all_to_all | solution.py:250
  32.3 1.9 %collective-permute-start = (bf16[8,16,8,128]{3,2,1,0:T(8,128)(2,1)S(1)}, bf16[8,16,8,128]{3,2,1,0:T(8,128)(2,1)S(1)}, u32[]{:S(2)}, u32[]{:S(2)}) collective-permute-start(bf16[8,16,8,128]{3,2,1,0:T(8,128)(2,1)S(1)} %slice.4), channel_id=1, source_target_pairs={{0,16},{16,0},{1,17},{17,1},{2,18},{18,2},{3,19},{19,3},{4,20},{20... | collective-permute-start | bytes 786440 | tf_op jit(solution)/shard_map/ppermute | solution.py:251
  34.3 1.0 shard_map.83
  35.3 0.2 collective-permute-done.other
  35.4 0.0 copy-start
  35.4 0.6 shard_map.84
  36.0 0.0 copy-start.1
  36.1 0.0 copy-start.2
  36.1 19.2 %all_to_all.21.y_ref = bf16[128,8,128]{2,1,0:T(8,128)(2,1)S(1)} all-to-all(bf16[128,8,128]{2,1,0:T(8,128)(2,1)S(1)} %bitcast.13), channel_id=1, replica_groups={{45,46,37,43,35,39,36,47,32,38,41,40,42,33,34,44,109,110,101,107,99,103..., dimensions={0} | all-to-all | bytes 524288 | tf_op jit(solution)/shard_map/all_to_all | solution.py:258
  55.2 0.0 copy-done
  55.2 0.0 copy-done.1
  55.2 0.0 copy-done.2
  55.2 1.4 %shard_map.85 = (f32[4,8,32,128]{3,2,1,0:T(8,128)S(1)}, bf16[128,16,128]{2,1,0:T(8,128)(2,1)S(1)}, bf16[8,128,128]{2,1,0:T(8,128)(2,1)S(1)}) custom-call(bf16[128,8,128]{2,1,0:T(8,128)(2,1)S(1)} %all_to_all.21.y_ref, f32[4,8,32,128]{3,2,1,0:T(8,128)S(1)} %bitcast.10, f32[8,128,128]{2,1,0:T(8,128)S(1)} %get-tuple-element.22.gate_ref, ...), custom_call_target="tpu_custom_call" | custom-call | tf_op jit(solution)/shard_map/pallas_call | solution.py:260
  56.6 23.3 %all_to_all.22 = bf16[128,16,128]{2,1,0:T(8,128)(2,1)S(1)} all-to-all(bf16[128,16,128]{2,1,0:T(8,128)(2,1)S(1)} %get-tuple-element.24), channel_id=1, replica_groups={{45,46,37,43,35,39,36,47,32,38,41,40,42,33,34,44,109,110,101,107,99,103..., dimensions={0} | all-to-all | bytes 1048576 | tf_op jit(solution)/shard_map/all_to_all | solution.py:269
  79.9 2.8 %collective-permute-start.1 = (bf16[8,16,16,128]{3,2,1,0:T(8,128)(2,1)S(1)}, bf16[8,16,16,128]{3,2,1,0:T(8,128)(2,1)S(1)}, u32[]{:S(2)}, u32[]{:S(2)}) collective-permute-start(bf16[8,16,16,128]{3,2,1,0:T(8,128)(2,1)S(1)} %bitcast.11), channel_id=1, source_target_pairs={{0,16},{16,0},{1,17},{17,1},{2,18},{18,2},{3,19},{19,3},{4,20},{20... | collective-permute-start | bytes 1572872 | tf_op jit(solution)/shard_map/ppermute | solution.py:270
  82.7 0.7 shard_map.86
  83.4 0.8 collective-permute-done.1.other
  84.3 0.8 shard_map.87
  85.1 19.0 %all_to_all.23.y_ref = bf16[128,8,128]{2,1,0:T(8,128)(2,1)S(1)} all-to-all(bf16[128,8,128]{2,1,0:T(8,128)(2,1)S(1)} %bitcast.14), channel_id=1, replica_groups={{45,46,37,43,35,39,36,47,32,38,41,40,42,33,34,44,109,110,101,107,99,103..., dimensions={0} | all-to-all | bytes 524288 | tf_op jit(solution)/shard_map/all_to_all | solution.py:275
  104.1 1.4 %shard_map.88 = f32[4,8,32,128]{3,2,1,0:T(8,128)} custom-call(bf16[128,8,128]{2,1,0:T(8,128)(2,1)S(1)} %all_to_all.23.y_ref, f32[4,8,32,128]{3,2,1,0:T(8,128)S(1)} %get-tuple-element.27.z_ref, f32[8,128,128]{2,1,0:T(8,128)S(1)} %get-tuple-element.28.gate_ref, f32[8,128]{1,0:T(8,128)S(1)} %get-tuple-element.23.vec, bf16[2,128,128]{2,1,0:T(8,128)(2,1)S(1)} %copy-done.2), custom_call_target="tpu_custom_call" | custom-call | tf_op jit(solution)/shard_map/pallas_call | solution.py:277
  (1 shorter events, 0.0 us)
Async XLA Ops:
  32.3 3.1 %collective-permute-start = (bf16[8,16,8,128]{3,2,1,0:T(8,128)(2,1)S(1)}, bf16[8,16,8,128]{3,2,1,0:T(8,128)(2,1)S(1)}, u32[]{:S(2)}, u32[]{:S(2)}) collective-permute-start(bf16[8,16,8,128]{3,2,1,0:T(8,128)(2,1)S(1)} %slice.4), channel_id=1, source_target_pairs={{0,16},{16,0},{1,17},{17,1},{2,18},{18,2},{3,19},{19,3},{4,20},{20... | collective-permute-start | bytes 786440 | tf_op jit(solution)/shard_map/ppermute | solution.py:251
  35.4 19.8 %copy-start = (f32[32,32,128]{2,1,0:T(8,128)S(1)}, f32[32,32,128]{2,1,0:T(8,128)}, u32[]{:S(2)}) copy-start(f32[32,32,128]{2,1,0:T(8,128)} %param.8) | copy-start | bytes 1572868
  36.0 19.2 %copy-start.1 = (bf16[2,128,512]{2,1,0:T(8,128)(2,1)S(1)}, bf16[2,128,512]{2,1,0:T(8,128)(2,1)}, u32[]{:S(2)}) copy-start(bf16[2,128,512]{2,1,0:T(8,128)(2,1)} %rest_0_.1) | copy-start | bytes 786436
  36.1 19.2 %copy-start.2 = (bf16[2,128,128]{2,1,0:T(8,128)(2,1)S(1)}, bf16[2,128,128]{2,1,0:T(8,128)(2,1)}, u32[]{:S(2)}) copy-start(bf16[2,128,128]{2,1,0:T(8,128)(2,1)} %out_w.3) | copy-start | bytes 196612
  79.9 4.3 %collective-permute-start.1 = (bf16[8,16,16,128]{3,2,1,0:T(8,128)(2,1)S(1)}, bf16[8,16,16,128]{3,2,1,0:T(8,128)(2,1)S(1)}, u32[]{:S(2)}, u32[]{:S(2)}) collective-permute-start(bf16[8,16,16,128]{3,2,1,0:T(8,128)(2,1)S(1)} %bitcast.11), channel_id=1, source_target_pairs={{0,16},{16,0},{1,17},{17,1},{2,18},{18,2},{3,19},{19,3},{4,20},{20... | collective-permute-start | bytes 1572872 | tf_op jit(solution)/shard_map/ppermute | solution.py:270
where the time goes:
time: 106 us; the launch traced here: 105 us
  blocking collectives  91.8 us (87%)
  Pallas kernels  7.8 us (7%)
  starting transfers between devices  4.73 us (4%)
    all_to_all x2, blocking collectives, local(): own = exchange(ops).reshape(8, 16, 16, 128)  53.6 us
    all_to_all x2, blocking collectives, local(): y = exchange(y.reshape(C, 8, 128))  38.2 us
    pallas_call x4, Pallas kernels, call(): pl.pallas_call(kernel, out_shape=outputs, in_specs=smem, out_specs=jax.tr...  3.12 us
    ppermute x1, starting transfers between devices, local(): other = lax.ppermute(own, 'core', swap)  2.79 us
  transfers between devices with their start and end apart: 2, of which 2 were waited for; matrix products, arithmetic and copies ran while one was open for 0% of the time, Pallas kernels for 2%

commit v1 on v0

--- a/solution.py
+++ b/solution.py
@@ -10,6 +10,7 @@
 RH_ORDER = (1, 3, 2, 7, 0, 6, 4, 5)
 COL_ORDER = (13, 14, 5, 11, 3, 7, 4, 15, 0, 6, 9, 8, 10, 1, 2, 12)
 RANKS = [8 * col + rh for rh in RH_ORDER for col in COL_ORDER]
+SENT = (jnp.float32, jnp.bfloat16)
 C = 128
 EPS = 1e-05
 VMEM_LIMIT = 48 * 1024 * 1024
@@ -77,7 +78,9 @@
     y32[...] = jnp.swapaxes(y_ref[...].astype(jnp.float32), 0, 1)
     gain = jnp.transpose(jnp.broadcast_to(vec[4 + layer : 5 + layer, :], (C, C)))
     bias = jnp.transpose(jnp.broadcast_to(vec[6 + layer : 7 + layer, :], (C, C)))
-    weight = jnp.concatenate([out_w[layer], out_w[layer]])
+    weight = out_w[layer]
+    if SENT[layer] == jnp.bfloat16:
+        weight = jnp.concatenate([weight, weight])
     copies = []
     for s in range(0, 8, 2):
         new = []
@@ -86,10 +89,10 @@
             centered = tile - jnp.mean(tile, axis=0, keepdims=True)
             scale = lax.rsqrt(jnp.mean(centered * centered, axis=0, keepdims=True) + EPS)
             normed = centered * scale * gain + bias
-            high = normed.astype(jnp.bfloat16)
-            low = (normed - high.astype(jnp.float32)).astype(jnp.bfloat16)
-            both = jnp.concatenate([high, low])
-            update = gate_ref[t] * dot(both, weight, ((0,), (0,)))
+            parts = [normed.astype(jnp.bfloat16)]
+            if SENT[layer] == jnp.bfloat16:
+                parts.append((normed - parts[0].astype(jnp.float32)).astype(jnp.bfloat16))
+            update = gate_ref[t] * dot(jnp.concatenate(parts), weight, ((0,), (0,)))
             value = z_ref[:, t] + update.reshape(4, 32, C)
             z_out[:, t] = value
             new.append(value)
@@ -122,7 +125,7 @@
 
 
 def write_back(product, b, y_ref):
-    for d, tile in enumerate(swap_groups([p.astype(jnp.bfloat16) for p in product])):
+    for d, tile in enumerate(swap_groups([p.astype(y_ref.dtype) for p in product])):
         y_ref[:, COL_ORDER.index(4 * b + d)] = tile.reshape(8, 8, 128)
 
 
@@ -144,7 +147,7 @@
     product = dot(left[...], rows, ((1,), (1,)))
     for b in range(2):
         parts = [product[64 * a : 64 * a + 64, 128 * b : 128 * b + 128] for a in range(4)]
-        for d, tile in enumerate(swap_groups([p.astype(jnp.bfloat16) for p in parts])):
+        for d, tile in enumerate(swap_groups([p.astype(SENT[0]) for p in parts])):
             put(4 * b + d, tile.reshape(8, 8, 128))
 
 
@@ -251,9 +254,9 @@
     other = lax.ppermute(own[:, :, 8:], "core", swap)
     half = 2 * 256 * 256 * 512
     rows = [pltpu.VMEM((8, 32, 512), jnp.float32)]
-    outputs = (shape((256, 512), jnp.bfloat16), shape((8, 8, 8, 128), jnp.bfloat16), gate_shape)
+    outputs = (shape((256, 512), jnp.bfloat16), shape((8, 8, 8, 128), SENT[0]), gate_shape)
     left, y_half, gate = call(outgoing_own, (own, normed, gate_w), outputs, rows, half)
-    outputs = shape((8, 16, 8, 128), jnp.bfloat16)
+    outputs = shape((8, 16, 8, 128), SENT[0])
     y = call(outgoing_other, (core, other, left, y_half), outputs, rows, half)
     y = exchange(y.reshape(C, 8, 128))
 
@@ -271,7 +274,7 @@
     sides = [pltpu.VMEM((256, 256), jnp.bfloat16), pltpu.VMEM((256, 512), jnp.bfloat16)]
     outputs = (shape((256, 512), jnp.float32), gate_shape)
     partial, gate = call(incoming_own, (core, own, normed, gate_w), outputs, sides, half)
-    y = call(incoming_other, (core, other, partial), shape((8, 16, 8, 128), jnp.bfloat16), sides, half)
+    y = call(incoming_other, (core, other, partial), shape((8, 16, 8, 128), SENT[1]), sides, half)
     y = exchange(y.reshape(C, 8, 128))
 
     out = pl.pallas_call(

time: 106 us -> 111 us (1.047)
  blocking collectives: 91.8 us -> 97.8 us
    all_to_all x2, blocking collectives: 38.2 us -> 44 us  [local(): y = exchange(y.reshape(C, 8, 128))]
where the time goes in v1:
time: 111 us
  blocking collectives  97.8 us (88%)
  Pallas kernels  7.93 us (7%)
  starting transfers between devices  4.39 us (4%)
    all_to_all x2, blocking collectives, local(): own = exchange(ops).reshape(8, 16, 16, 128)  53.8 us
    all_to_all x2, blocking collectives, local(): y = exchange(y.reshape(C, 8, 128))  44 us
    pallas_call x4, Pallas kernels, call(): pl.pallas_call(kernel, out_shape=outputs, in_specs=smem, out_specs=jax.tr...  3.21 us
    ppermute x1, starting transfers between devices, local(): other = lax.ppermute(own, 'core', swap)  2.45 us
  transfers between devices with their start and end apart: 2, of which 2 were waited for; matrix products, arithmetic and copies ran while one was open for 0% of the time, Pallas kernels for 2%

profile of v1, /device:TPU:1, one launch (start us, length us, event | category | flops | bytes accessed | tf_op | source)
XLA Modules:
  0.0 111.2 jit_solution(17428165035429468676)
XLA Ops:
  0.0 1.9 %shard_map.82 = (bf16[128,16,128]{2,1,0:T(8,128)(2,1)S(1)}, bf16[8,128,128]{2,1,0:T(8,128)(2,1)S(1)}, f32[8,128]{1,0:T(8,128)S(1)}, bf16[2,128,128]{2,1,0:T(8,128)(2,1)S(1)}) custom-call(f32[4,8,32,128]{3,2,1,0:T(8,128)} %bitcast.12, f32[2,128]{1,0:T(2,128)} %gain_in.1, f32[2,128]{1,0:T(2,128)} %bias_in.1, bf16[2,128,512]{2,1,0:T(8,128)(2,1)} %rest_0_.1, ...), custom_call_target="tpu_custom_call" | custom-call | tf_op jit(solution)/shard_map/pallas_call | solution.py:239
  1.9 30.3 %all_to_all.20 = bf16[128,16,128]{2,1,0:T(8,128)(2,1)S(1)} all-to-all(bf16[128,16,128]{2,1,0:T(8,128)(2,1)S(1)} %get-tuple-element.17), channel_id=1, replica_groups={{45,46,37,43,35,39,36,47,32,38,41,40,42,33,34,44,109,110,101,107,99,103..., dimensions={0} | all-to-all | bytes 1048576 | tf_op jit(solution)/shard_map/all_to_all | solution.py:253
  32.3 1.9 %collective-permute-start = (bf16[8,16,8,128]{3,2,1,0:T(8,128)(2,1)S(1)}, bf16[8,16,8,128]{3,2,1,0:T(8,128)(2,1)S(1)}, u32[]{:S(2)}, u32[]{:S(2)}) collective-permute-start(bf16[8,16,8,128]{3,2,1,0:T(8,128)(2,1)S(1)} %slice.4), channel_id=1, source_target_pairs={{0,16},{16,0},{1,17},{17,1},{2,18},{18,2},{3,19},{19,3},{4,20},{20... | collective-permute-start | bytes 786440 | tf_op jit(solution)/shard_map/ppermute | solution.py:254
  34.3 1.1 shard_map.83
  35.4 0.1 collective-permute-done.other
  35.4 0.6 shard_map.84
  36.1 0.0 copy-start
  36.1 0.0 copy-start.1
  36.1 0.0 copy-start.2
  36.1 24.9 %all_to_all.21.y_ref = f32[128,8,128]{2,1,0:T(8,128)S(1)} all-to-all(f32[128,8,128]{2,1,0:T(8,128)S(1)} %bitcast.9), channel_id=1, replica_groups={{45,46,37,43,35,39,36,47,32,38,41,40,42,33,34,44,109,110,101,107,99,103..., dimensions={0} | all-to-all | bytes 1048576 | tf_op jit(solution)/shard_map/all_to_all | solution.py:261
  61.0 0.0 copy-done
  61.0 0.0 copy-done.1
  61.0 0.0 copy-done.2
  61.0 1.4 %shard_map.85 = (f32[4,8,32,128]{3,2,1,0:T(8,128)S(1)}, bf16[128,16,128]{2,1,0:T(8,128)(2,1)S(1)}, bf16[8,128,128]{2,1,0:T(8,128)(2,1)S(1)}) custom-call(f32[128,8,128]{2,1,0:T(8,128)S(1)} %all_to_all.21.y_ref, f32[4,8,32,128]{3,2,1,0:T(8,128)S(1)} %bitcast.13, f32[8,128,128]{2,1,0:T(8,128)S(1)} %get-tuple-element.22.gate_ref, ...), custom_call_target="tpu_custom_call" | custom-call | tf_op jit(solution)/shard_map/pallas_call | solution.py:263
  62.5 23.5 %all_to_all.22 = bf16[128,16,128]{2,1,0:T(8,128)(2,1)S(1)} all-to-all(bf16[128,16,128]{2,1,0:T(8,128)(2,1)S(1)} %get-tuple-element.24), channel_id=1, replica_groups={{45,46,37,43,35,39,36,47,32,38,41,40,42,33,34,44,109,110,101,107,99,103..., dimensions={0} | all-to-all | bytes 1048576 | tf_op jit(solution)/shard_map/all_to_all | solution.py:272
  86.0 2.4 %collective-permute-start.1 = (bf16[8,16,16,128]{3,2,1,0:T(8,128)(2,1)S(1)}, bf16[8,16,16,128]{3,2,1,0:T(8,128)(2,1)S(1)}, u32[]{:S(2)}, u32[]{:S(2)}) collective-permute-start(bf16[8,16,16,128]{3,2,1,0:T(8,128)(2,1)S(1)} %bitcast.10), channel_id=1, source_target_pairs={{0,16},{16,0},{1,17},{17,1},{2,18},{18,2},{3,19},{19,3},{4,20},{20... | collective-permute-start | bytes 1572872 | tf_op jit(solution)/shard_map/ppermute | solution.py:273
  88.4 0.7 shard_map.86
  89.1 0.8 collective-permute-done.1.other
  89.9 0.8 shard_map.87
  90.8 19.1 %all_to_all.23.y_ref = bf16[128,8,128]{2,1,0:T(8,128)(2,1)S(1)} all-to-all(bf16[128,8,128]{2,1,0:T(8,128)(2,1)S(1)} %bitcast.14), channel_id=1, replica_groups={{45,46,37,43,35,39,36,47,32,38,41,40,42,33,34,44,109,110,101,107,99,103..., dimensions={0} | all-to-all | bytes 524288 | tf_op jit(solution)/shard_map/all_to_all | solution.py:278
  109.8 1.3 %shard_map.88 = f32[4,8,32,128]{3,2,1,0:T(8,128)} custom-call(bf16[128,8,128]{2,1,0:T(8,128)(2,1)S(1)} %all_to_all.23.y_ref, f32[4,8,32,128]{3,2,1,0:T(8,128)S(1)} %get-tuple-element.27.z_ref, f32[8,128,128]{2,1,0:T(8,128)S(1)} %get-tuple-element.28.gate_ref, f32[8,128]{1,0:T(8,128)S(1)} %get-tuple-element.23.vec, bf16[2,128,128]{2,1,0:T(8,128)(2,1)S(1)} %copy-done.2), custom_call_target="tpu_custom_call" | custom-call | tf_op jit(solution)/shard_map/pallas_call | solution.py:280
  (1 shorter events, 0.0 us)
Async XLA Ops:
  32.3 3.1 %collective-permute-start = (bf16[8,16,8,128]{3,2,1,0:T(8,128)(2,1)S(1)}, bf16[8,16,8,128]{3,2,1,0:T(8,128)(2,1)S(1)}, u32[]{:S(2)}, u32[]{:S(2)}) collective-permute-start(bf16[8,16,8,128]{3,2,1,0:T(8,128)(2,1)S(1)} %slice.4), channel_id=1, source_target_pairs={{0,16},{16,0},{1,17},{17,1},{2,18},{18,2},{3,19},{19,3},{4,20},{20... | collective-permute-start | bytes 786440 | tf_op jit(solution)/shard_map/ppermute | solution.py:254
  36.1 25.0 %copy-start = (f32[32,32,128]{2,1,0:T(8,128)S(1)}, f32[32,32,128]{2,1,0:T(8,128)}, u32[]{:S(2)}) copy-start(f32[32,32,128]{2,1,0:T(8,128)} %param.8) | copy-start | bytes 1572868
  36.1 25.0 %copy-start.1 = (bf16[2,128,512]{2,1,0:T(8,128)(2,1)S(1)}, bf16[2,128,512]{2,1,0:T(8,128)(2,1)}, u32[]{:S(2)}) copy-start(bf16[2,128,512]{2,1,0:T(8,128)(2,1)} %rest_0_.1) | copy-start | bytes 786436
  36.1 24.9 %copy-start.2 = (bf16[2,128,128]{2,1,0:T(8,128)(2,1)S(1)}, bf16[2,128,128]{2,1,0:T(8,128)(2,1)}, u32[]{:S(2)}) copy-start(bf16[2,128,128]{2,1,0:T(8,128)(2,1)} %out_w.3) | copy-start | bytes 196612
  86.0 4.0 %collective-permute-start.1 = (bf16[8,16,16,128]{3,2,1,0:T(8,128)(2,1)S(1)}, bf16[8,16,16,128]{3,2,1,0:T(8,128)(2,1)S(1)}, u32[]{:S(2)}, u32[]{:S(2)}) collective-permute-start(bf16[8,16,16,128]{3,2,1,0:T(8,128)(2,1)S(1)} %bitcast.10), channel_id=1, source_target_pairs={{0,16},{16,0},{1,17},{17,1},{2,18},{18,2},{3,19},{19,3},{4,20},{20... | collective-permute-start | bytes 1572872 | tf_op jit(solution)/shard_map/ppermute | solution.py:273

commit v2 on v1

--- a/solution.py
+++ b/solution.py
@@ -7,7 +7,7 @@
 from jax.experimental.pallas import tpu as pltpu
 from jax.sharding import Mesh, PartitionSpec as P
 
-RH_ORDER = (1, 3, 2, 7, 0, 6, 4, 5)
+RH_ORDER = (1, 3, 7, 2, 6, 0, 4, 5)
 COL_ORDER = (13, 14, 5, 11, 3, 7, 4, 15, 0, 6, 9, 8, 10, 1, 2, 12)
 RANKS = [8 * col + rh for rh in RH_ORDER for col in COL_ORDER]
 SENT = (jnp.float32, jnp.bfloat16)
@@ -62,12 +62,14 @@
     copies = [pltpu.make_async_copy(src, dst, sems.at[i]) for i, (src, dst) in enumerate(pairs)]
     for copy in copies:
         copy.start()
-    for copy in copies:
+    for copy in copies[:4]:
         copy.wait()
     for s in range(0, 8, 2):
         rows = jnp.stack([z[:, s], z[:, s + 1]])
         emit_operands(rows, s, vec_ref[0:1], vec_ref[2:3], proj[...], wide, normed_ref)
     ops_ref[...] = jnp.swapaxes(wide[...], 0, 1)
+    for copy in copies[4:]:
+        copy.wait()
 
 
 def finish_kernel(layer, y_ref, z_ref, gate_ref, vec, out_w, *rest):

time: 111 us -> 111 us (level)
  no operation moved by 1% of the time
where the time goes in v2:
time: 111 us
  blocking collectives  97.2 us (88%)
  Pallas kernels  7.92 us (7%)
  starting transfers between devices  4.8 us (4%)
    all_to_all x2, blocking collectives, local(): own = exchange(ops).reshape(8, 16, 16, 128)  53.3 us
    all_to_all x2, blocking collectives, local(): y = exchange(y.reshape(C, 8, 128))  43.9 us
    pallas_call x4, Pallas kernels, call(): pl.pallas_call(kernel, out_shape=outputs, in_specs=smem, out_specs=jax.tr...  3.23 us
    ppermute x1, starting transfers between devices, local(): other = lax.ppermute(own, 'core', swap)  2.64 us
  transfers between devices with their start and end apart: 2, of which 2 were waited for; matrix products, arithmetic and copies ran while one was open for 0% of the time, Pallas kernels for 2%

profile of v2, /device:TPU:1, one launch (start us, length us, event | category | flops | bytes accessed | tf_op | source)
XLA Modules:
  0.0 111.0 jit_solution(7308396961915636717)
XLA Ops:
  0.0 1.9 %shard_map.82 = (bf16[128,16,128]{2,1,0:T(8,128)(2,1)S(1)}, bf16[8,128,128]{2,1,0:T(8,128)(2,1)S(1)}, f32[8,128]{1,0:T(8,128)S(1)}, bf16[2,128,128]{2,1,0:T(8,128)(2,1)S(1)}) custom-call(f32[4,8,32,128]{3,2,1,0:T(8,128)} %bitcast.12, f32[2,128]{1,0:T(2,128)} %gain_in.1, f32[2,128]{1,0:T(2,128)} %bias_in.1, bf16[2,128,512]{2,1,0:T(8,128)(2,1)} %rest_0_.1, ...), custom_call_target="tpu_custom_call" | custom-call | tf_op jit(solution)/shard_map/pallas_call | solution.py:241
  1.9 29.8 %all_to_all.20 = bf16[128,16,128]{2,1,0:T(8,128)(2,1)S(1)} all-to-all(bf16[128,16,128]{2,1,0:T(8,128)(2,1)S(1)} %get-tuple-element.17), channel_id=1, replica_groups={{45,46,37,43,35,39,36,47,32,38,41,40,42,33,34,44,109,110,101,107,99,103..., dimensions={0} | all-to-all | bytes 1048576 | tf_op jit(solution)/shard_map/all_to_all | solution.py:255
  31.8 2.2 %collective-permute-start = (bf16[8,16,8,128]{3,2,1,0:T(8,128)(2,1)S(1)}, bf16[8,16,8,128]{3,2,1,0:T(8,128)(2,1)S(1)}, u32[]{:S(2)}, u32[]{:S(2)}) collective-permute-start(bf16[8,16,8,128]{3,2,1,0:T(8,128)(2,1)S(1)} %slice.4), channel_id=1, source_target_pairs={{0,16},{16,0},{1,17},{17,1},{2,18},{18,2},{3,19},{19,3},{4,20},{20... | collective-permute-start | bytes 786440 | tf_op jit(solution)/shard_map/ppermute | solution.py:256
  34.0 1.1 shard_map.83
  35.0 0.1 collective-permute-done.other
  35.1 0.6 shard_map.84
  35.7 0.0 copy-start
  35.8 0.0 copy-start.1
  35.8 0.0 copy-start.2
  35.8 24.7 %all_to_all.21.y_ref = f32[128,8,128]{2,1,0:T(8,128)S(1)} all-to-all(f32[128,8,128]{2,1,0:T(8,128)S(1)} %bitcast.9), channel_id=1, replica_groups={{45,46,37,43,35,39,36,47,32,38,41,40,42,33,34,44,109,110,101,107,99,103..., dimensions={0} | all-to-all | bytes 1048576 | tf_op jit(solution)/shard_map/all_to_all | solution.py:263
  60.5 0.0 copy-done
  60.5 0.0 copy-done.1
  60.5 0.0 copy-done.2
  60.5 1.4 %shard_map.85 = (f32[4,8,32,128]{3,2,1,0:T(8,128)S(1)}, bf16[128,16,128]{2,1,0:T(8,128)(2,1)S(1)}, bf16[8,128,128]{2,1,0:T(8,128)(2,1)S(1)}) custom-call(f32[128,8,128]{2,1,0:T(8,128)S(1)} %all_to_all.21.y_ref, f32[4,8,32,128]{3,2,1,0:T(8,128)S(1)} %bitcast.13, f32[8,128,128]{2,1,0:T(8,128)S(1)} %get-tuple-element.22.gate_ref, ...), custom_call_target="tpu_custom_call" | custom-call | tf_op jit(solution)/shard_map/pallas_call | solution.py:265
  61.9 23.5 %all_to_all.22 = bf16[128,16,128]{2,1,0:T(8,128)(2,1)S(1)} all-to-all(bf16[128,16,128]{2,1,0:T(8,128)(2,1)S(1)} %get-tuple-element.24), channel_id=1, replica_groups={{45,46,37,43,35,39,36,47,32,38,41,40,42,33,34,44,109,110,101,107,99,103..., dimensions={0} | all-to-all | bytes 1048576 | tf_op jit(solution)/shard_map/all_to_all | solution.py:274
  85.4 2.6 %collective-permute-start.1 = (bf16[8,16,16,128]{3,2,1,0:T(8,128)(2,1)S(1)}, bf16[8,16,16,128]{3,2,1,0:T(8,128)(2,1)S(1)}, u32[]{:S(2)}, u32[]{:S(2)}) collective-permute-start(bf16[8,16,16,128]{3,2,1,0:T(8,128)(2,1)S(1)} %bitcast.10), channel_id=1, source_target_pairs={{0,16},{16,0},{1,17},{17,1},{2,18},{18,2},{3,19},{19,3},{4,20},{20... | collective-permute-start | bytes 1572872 | tf_op jit(solution)/shard_map/ppermute | solution.py:275
  88.1 0.7 shard_map.86
  88.8 0.8 collective-permute-done.1.other
  89.6 0.8 shard_map.87
  90.5 19.2 %all_to_all.23.y_ref = bf16[128,8,128]{2,1,0:T(8,128)(2,1)S(1)} all-to-all(bf16[128,8,128]{2,1,0:T(8,128)(2,1)S(1)} %bitcast.14), channel_id=1, replica_groups={{45,46,37,43,35,39,36,47,32,38,41,40,42,33,34,44,109,110,101,107,99,103..., dimensions={0} | all-to-all | bytes 524288 | tf_op jit(solution)/shard_map/all_to_all | solution.py:280
  109.6 1.3 %shard_map.88 = f32[4,8,32,128]{3,2,1,0:T(8,128)} custom-call(bf16[128,8,128]{2,1,0:T(8,128)(2,1)S(1)} %all_to_all.23.y_ref, f32[4,8,32,128]{3,2,1,0:T(8,128)S(1)} %get-tuple-element.27.z_ref, f32[8,128,128]{2,1,0:T(8,128)S(1)} %get-tuple-element.28.gate_ref, f32[8,128]{1,0:T(8,128)S(1)} %get-tuple-element.23.vec, bf16[2,128,128]{2,1,0:T(8,128)(2,1)S(1)} %copy-done.2), custom_call_target="tpu_custom_call" | custom-call | tf_op jit(solution)/shard_map/pallas_call | solution.py:282
  (1 shorter events, 0.0 us)
Async XLA Ops:
  31.8 3.3 %collective-permute-start = (bf16[8,16,8,128]{3,2,1,0:T(8,128)(2,1)S(1)}, bf16[8,16,8,128]{3,2,1,0:T(8,128)(2,1)S(1)}, u32[]{:S(2)}, u32[]{:S(2)}) collective-permute-start(bf16[8,16,8,128]{3,2,1,0:T(8,128)(2,1)S(1)} %slice.4), channel_id=1, source_target_pairs={{0,16},{16,0},{1,17},{17,1},{2,18},{18,2},{3,19},{19,3},{4,20},{20... | collective-permute-start | bytes 786440 | tf_op jit(solution)/shard_map/ppermute | solution.py:256
  35.7 24.8 %copy-start = (f32[32,32,128]{2,1,0:T(8,128)S(1)}, f32[32,32,128]{2,1,0:T(8,128)}, u32[]{:S(2)}) copy-start(f32[32,32,128]{2,1,0:T(8,128)} %param.8) | copy-start | bytes 1572868
  35.8 24.7 %copy-start.1 = (bf16[2,128,512]{2,1,0:T(8,128)(2,1)S(1)}, bf16[2,128,512]{2,1,0:T(8,128)(2,1)}, u32[]{:S(2)}) copy-start(bf16[2,128,512]{2,1,0:T(8,128)(2,1)} %rest_0_.1) | copy-start | bytes 786436
  35.8 24.7 %copy-start.2 = (bf16[2,128,128]{2,1,0:T(8,128)(2,1)S(1)}, bf16[2,128,128]{2,1,0:T(8,128)(2,1)}, u32[]{:S(2)}) copy-start(bf16[2,128,128]{2,1,0:T(8,128)(2,1)} %out_w.3) | copy-start | bytes 196612
  85.4 4.2 %collective-permute-start.1 = (bf16[8,16,16,128]{3,2,1,0:T(8,128)(2,1)S(1)}, bf16[8,16,16,128]{3,2,1,0:T(8,128)(2,1)S(1)}, u32[]{:S(2)}, u32[]{:S(2)}) collective-permute-start(bf16[8,16,16,128]{3,2,1,0:T(8,128)(2,1)S(1)} %bitcast.10), channel_id=1, source_target_pairs={{0,16},{16,0},{1,17},{17,1},{2,18},{18,2},{3,19},{19,3},{4,20},{20... | collective-permute-start | bytes 1572872 | tf_op jit(solution)/shard_map/ppermute | solution.py:275
